TPU v7x, 32 devices: a whole 2x2x4 slice. The times are simulated.
32 devices in a mesh: grp: 2 (over y), freq: 4 (over z), shot: 2 (over x), rcv: 2 (over core).
Axes of the slice: x: 2, y: 2, z: 4, core: 2. Of those that a mesh axis runs over, the one named last changes fastest.
Arguments:
- data: bfloat16 [2, 256, 32, 4096], P(None, 'freq', ('grp', 'shot'), 'rcv'), parts along dimension 2, may hold values from -6 to 6
- estimate: bfloat16 [2, 256, 32, 4096], P(None, 'freq', ('grp', 'shot'), 'rcv'), parts along dimension 2, may hold values from -0.09375 to 0.09375
- window_data: bfloat16 [2, 256, 32, 16], P(None, 'freq', ('grp', 'shot')), parts along dimension 2, may hold values from -6 to 6
- wavelet: float32 [2, 512], P(None, ('grp', 'freq')), parts along dimension 1, may hold values from -24 to 24
- positions: int32 [32], P(('grp', 'shot')), parts along dimension 0, may hold values from 0 to 4095
- bins: int32 [512], P('grp'), parts along dimension 0, may hold values from 0 to 399
- threshold: int32 [2], P('grp'), parts along dimension 0, may hold values from 8 to 40
- step: float32 [2], P('grp'), parts along dimension 0, may hold values from 0.25 to 1
Outputs:
- primaries: bfloat16 [1024, 32, 4096], P('freq', ('grp', 'shot'), 'rcv'), parts along dimension 1
There are 2 independent parts, one for each index of `grp`. A program takes and returns all parts, laid end to end along the dimension named above; each array names one. Nothing has to cross between parts.
All inputs are finite; a program needn't handle non-finite values.
Results may differ from a plain program's by a relative error of at most 0.0059.
The roundings to bfloat16 on the way count: a program that leaves them out, or rounds other values in their place, can miss the bound.
Values may be sent and summed in bfloat16 or wider, within the bound.
A program may use at most 64 MiB of HBM per device.

v0:
```python
from functools import partial
import math
import jax
import jax.numpy as jnp
from jax import lax
from jax.sharding import PartitionSpec as P

NF = 256
RCV = 4096
NT = 1024


def make_down(lines, spots, wavelet, offset):
    width = lines.shape[3]
    columns = offset + lax.iota(jnp.int32, width)
    select = (columns[None, None, :] == spots[None, :, None]).astype(jnp.float32)
    down_re = (wavelet[0][:, None, None] * select - lines[0].astype(jnp.float32)).astype(
        jnp.bfloat16
    )
    down_im = (wavelet[1][:, None, None] * select - lines[1].astype(jnp.float32)).astype(
        jnp.bfloat16
    )
    return (down_re, down_im)


def body(data, estimate, window_data, wavelet, positions, bins, threshold, step):
    product = partial(jnp.einsum, preferred_element_type=jnp.float32)
    offset = lax.axis_index("rcv") * data.shape[3]
    shots_all = data.shape[2] * lax.axis_size("shot")
    norm = 1.0 / math.sqrt(shots_all * RCV)
    lines, spots = (
        lax.all_gather(data, "shot", axis=2, tiled=True),
        lax.all_gather(positions, "shot", axis=0, tiled=True),
    )
    down_re, down_im = make_down(lines, spots, wavelet, offset)
    rows_re = estimate[0]
    rows_im = estimate[1]
    model_re = product("frc,fsc->frs", rows_re, down_re) - product("frc,fsc->frs", rows_im, down_im)
    model_im = product("frc,fsc->frs", rows_re, down_im) + product("frc,fsc->frs", rows_im, down_re)
    model_re, model_im = lax.psum((model_re, model_im), "rcv")
    err_re = (window_data[0].astype(jnp.float32) - model_re).astype(jnp.bfloat16)
    err_im = (window_data[1].astype(jnp.float32) - model_im).astype(jnp.bfloat16)
    grad_re = product("frs,fsc->frc", err_re, down_re) + product("frs,fsc->frc", err_im, down_im)
    grad_im = product("frs,fsc->frc", err_im, down_re) - product("frs,fsc->frc", err_re, down_im)
    step_size = step[0]
    upd_re = (estimate[0].astype(jnp.float32) - step_size * (grad_re * norm)).astype(jnp.bfloat16)
    upd_im = (estimate[1].astype(jnp.float32) - step_size * (grad_im * norm)).astype(jnp.bfloat16)
    updated = jnp.stack([upd_re, upd_im], axis=0)
    n_freq = bins.shape[0]
    times = lax.iota(jnp.int32, NT)
    phase = bins[:, None] * times[None, :] % NT
    angle = 2.0 * math.pi / NT * phase.astype(jnp.float32)
    table = jnp.concatenate([jnp.cos(angle), -jnp.sin(angle)], axis=0).astype(jnp.bfloat16)
    level = threshold[0].astype(jnp.float32) / 64.0
    amplitude = math.sqrt(RCV / NF)
    piece = lax.all_to_all(updated, "freq", split_axis=3, concat_axis=1, tiled=True)
    row_count = piece.shape[2]
    col_count = piece.shape[3]
    stacked = piece.reshape(2 * n_freq, row_count * col_count)
    trace = (
        lax.dot_general(
            table, stacked, (((0,), (0,)), ((), ())), preferred_element_type=jnp.float32
        )
        * amplitude
    )
    sparse = (jnp.sign(trace) * jnp.maximum(jnp.abs(trace) - level, 0.0)).astype(jnp.bfloat16)
    sparse = sparse.reshape(NT, row_count, col_count)
    return lax.all_to_all(sparse, "freq", split_axis=0, concat_axis=2, tiled=True)


def solution(mesh):
    return jax.shard_map(
        body,
        mesh=mesh,
        in_specs=(
            P(None, "freq", ("grp", "shot"), "rcv"),
            P(None, "freq", ("grp", "shot"), "rcv"),
            P(None, "freq", ("grp", "shot"), None),
            P(None, ("grp", "freq")),
            P(("grp", "shot")),
            P("grp"),
            P("grp"),
            P("grp"),
        ),
        out_specs=P("freq", ("grp", "shot"), "rcv"),
        check_vma=False,
    )
```

profile of v0, /device:TPU:0, one launch (start us, length us, event | category | flops | bytes accessed | tf_op | source)
XLA Modules:
  0.0 535.6 jit_solution(10995999869594317697)
XLA Ops:
  6.5 0.0 copy-start.12
  6.5 0.0 copy-start.11
  6.5 0.0 copy-start.10
  6.5 0.0 all-gather.2.cloned.1.call-start
  6.5 0.7 all-gather.2.cloned.1.call-update
  7.3 0.0 all-reduce.4.cloned.1.call-start
  7.3 0.0 copy-done.12
  7.3 0.6 dynamic-slice
  8.6 0.0 copy-done.11
  8.6 0.2 dynamic-update-slice
  8.8 5.2 all-reduce
  14.0 0.0 copy-done.10
  14.0 0.1 compare_convert_fusion
  14.1 101.5 %all-gather.2.cloned.1.call-done = bf16[2,64,16,2048]{3,2,1,0:T(8,128)(2,1)} async-done(((bf16[2,64,8,2048]{3,2,1,0:T(8,128)(2,1)}), bf16[2,64,16,2048]{3,2,1,0:T(8,128)(2,1)}) %all-gather.2.cloned.1.call-update) | async-done | bytes 8388624 | tf_op jit(solution)/shard_map/all_gather | solution.py:32
  115.6 0.0 copy-start.4
  115.6 5.3 fusion
  121.0 0.0 copy-start.2
  121.0 0.0 copy-start
  121.0 0.0 copy-done.4
  121.0 1.6 fusion.6
  122.6 1.6 fusion.4
  124.1 0.0 copy-done.2
  124.1 2.3 fusion.19
  126.4 0.0 copy-done
  126.4 0.0 copy-start.8
  126.4 1.9 fusion.25
  128.3 0.0 all-reduce.4.cloned.1.call-update
  128.4 0.0 copy-done.8
  128.4 0.1 copy.26
  128.5 0.1 copy.27
  129.3 18.0 %all-reduce.4.cloned.1.call-done = (f32[64,8,16]{2,1,0:T(8,128)}, f32[64,8,16]{2,1,0:T(8,128)}) async-done(((f32[64,8,16]{2,1,0:T(8,128)}, f32[64,8,16]{2,1,0:T(8,128)}), (f32[64,8,16]{2,1,0:T(8,128)}, f32[64,8,16]{2,1,0:T(8,128)})) %all-reduce.4.cloned.1.call-update) | async-done | bytes 65552 | tf_op jit(solution)/shard_map/psum | solution.py:40
  147.3 0.0 copy-start.3
  147.3 0.0 copy-start.7
  147.3 3.1 fusion.41
  150.4 0.4 copy-done.3
  150.8 0.0 copy-done.7
  150.9 0.0 copy-start.1
  150.9 0.0 copy-start.5
  150.9 0.7 fusion.43
  151.6 1.5 copy-done.1
  153.1 1.3 copy-done.5
  154.3 0.0 copy-start.6
  154.3 1.0 fusion.2
  155.3 0.0 copy-done.6
  155.3 1.0 fusion.3
  156.3 2.3 pad_maximum_fusion
  158.6 13.2 %copy.23 = bf16[2,64,8,2048]{1,2,0,3:T(8,128)(2,1)} copy(bf16[2,64,8,2048]{3,2,1,0:T(8,128)(2,1)} %pad_maximum_fusion) | data formatting | bytes 8388608 | tf_op jit(solution)/shard_map/stack | solution.py:48
  171.8 9.6 %reshape.71 = bf16[4,2,262144]{2,1,0:T(2,128)(2,1)} reshape(bf16[2048,2,8,64]{3,2,1,0:T(8,128)(2,1)} %bitcast.77) | data formatting | bytes 8388608
  181.4 0.0 copy-start.9
  181.4 5.0 all-to-all-start
  187.0 0.0 copy-done.9
  187.1 4.9 cosine_convert_fusion
  191.9 88.4 %all-to-all-done = bf16[4,2,262144]{2,1,0:T(2,128)(2,1)} async-done(((bf16[4,2,262144]{2,1,0:T(2,128)(2,1)}), bf16[4,2,262144]{2,1,0:T(2,128)(2,1)}, u32[]{:S(2)}, u32[]{:S(2)}) %all-to-all-start) | async-done | bytes 4194336 | tf_op jit(solution)/shard_map/all_to_all | solution.py:56
  280.3 9.3 %reshape.72 = bf16[2048,2,8,64]{3,2,1,0:T(8,128)(2,1)} reshape(bf16[4,2,262144]{2,1,0:T(2,128)(2,1)} %all-to-all-done) | data formatting | bytes 8388608
  289.6 12.0 %copy.24 = bf16[2,64,8,4,512]{4,2,1,3,0:T(8,128)(2,1)} copy(bf16[2,64,8,4,512]{1,2,0,4,3:T(8,128)(2,1)} %bitcast.78) | data formatting | bytes 8388608 | tf_op jit(solution)/shard_map/all_to_all | solution.py:56
  301.6 4.4 copy.28
  306.0 12.1 %multiply_convert_fusion = bf16[1024,4096]{1,0:T(8,128)(2,1)} fusion(bf16[512,4096]{1,0:T(8,128)(2,1)S(1)} %bitcast.83, f32[]{:T(128)} %bitcast.16, bf16[256,1024]{1,0:T(8,128)(2,1)S(1)} %get-tuple-element.12, bf16[256,1024]{1,0:T(8,128)(2,1)S(1)} %get-tuple-element.11), kind=kOutput, calls=%fused_computation | convolution fusion | flops 4326424576 | bytes 13631492 | tf_op jit(solution)/shard_map/dot_general | solution.py:61
  318.1 12.2 %copy.29 = bf16[128,8,8,512]{3,2,1,0:T(8,128)(2,1)} copy(bf16[128,8,8,512]{3,1,2,0:T(8,128)(2,1)} %bitcast.82) | data formatting | bytes 16777216
  330.3 190.4 %all_to_all.33 = bf16[1024,8,512]{2,1,0:T(8,128)(2,1)} all-to-all(bf16[1024,8,512]{2,1,0:T(8,128)(2,1)} %bitcast.79), channel_id=1, replica_groups=mesh['grp'=2,'freq'=4,'shot'=2,'rcv'=2] {'freq'}, dimensions={0} | all-to-all | bytes 16777216 | tf_op jit(solution)/shard_map/all_to_all | solution.py:68
  520.7 8.1 %copy.25 = bf16[4,256,8,512]{3,2,0,1:T(8,128)(2,1)} copy(bf16[4,256,8,512]{3,2,1,0:T(8,128)(2,1)} %bitcast.80) | data formatting | bytes 16777216 | tf_op jit(solution)/shard_map/all_to_all | solution.py:68
  (4 shorter events, 0.0 us)
Async XLA Ops:
  6.5 0.8 copy-start.12
  6.5 2.0 copy-start.11
  6.5 7.5 %copy-start.10 = (f32[2,64]{1,0:T(2,128)S(1)}, f32[2,64]{1,0:T(2,128)}, u32[]{:S(2)}) copy-start(f32[2,64]{1,0:T(2,128)} %param.11) | copy-start | bytes 1540
  6.5 109.1 %all-gather.2.cloned.1.call-start = ((), (), s32[]{:S(2)}) async-start(), calls=%async_computation.2 | async-start | bytes 12582912 | tf_op jit(solution)/shard_map/all_gather | solution.py:32
  7.3 140.1 %all-reduce.4.cloned.1.call-start = ((), (), s32[]{:S(2)}) async-start(), calls=%async_computation.3 | async-start | bytes 1048576 | tf_op jit(solution)/shard_map/psum | solution.py:40
  115.6 5.3 copy-start.4
  121.0 3.2 copy-start.2
  121.0 5.5 %copy-start = (bf16[64,16,2048]{2,1,0:T(8,128)(2,1)}, bf16[64,16,2048]{2,1,0:T(8,128)(2,1)S(1)}, u32[]{:S(2)}) copy-start(bf16[64,16,2048]{2,1,0:T(8,128)(2,1)S(1)} %get-tuple-element.7) | copy-start | bytes 12582916
  126.4 1.9 copy-start.8
  147.3 3.5 copy-start.3
  147.3 3.5 copy-start.7
  150.9 2.2 copy-start.1
  150.9 3.5 copy-start.5
  154.3 1.0 copy-start.6
  181.4 5.7 %copy-start.9 = (s32[256]{0:T(256)S(1)}, s32[256]{0:T(256)}, u32[]{:S(2)}) copy-start(s32[256]{0:T(256)} %param.13) | copy-start | bytes 3076
  181.4 99.0 %all-to-all-start = ((bf16[4,2,262144]{2,1,0:T(2,128)(2,1)}), bf16[4,2,262144]{2,1,0:T(2,128)(2,1)}, u32[]{:S(2)}, u32[]{:S(2)}) async-start(bf16[4,2,262144]{2,1,0:T(2,128)(2,1)} %reshape.71), calls=%async_computation | async-start | bytes 8388608 | tf_op jit(solution)/shard_map/all_to_all | solution.py:56
Sparse Core Ops, SparseCore 0:
  8.9 106.6 all-gather.1
  128.5 18.7 all-reduce.3
where the time goes:
time: 537 us; the launch traced here: 536 us
  waiting for transfers between devices  209 us (39%)
  blocking collectives  196 us (36%)
  local copies, waits for them, and re-layouts  73.1 us (14%)
  matrix products  25.2 us (5%)
  between operations  15.5 us (3%)
  other arithmetic  12.6 us (2%)
    all_to_all x1, blocking collectives, body(): lax.all_to_all(sparse, 'freq', split_axis=0, concat_axis=2, tiled=True)  190 us
    all_gather x1, waiting for transfers between devices, body(): lax.all_gather(data, 'shot', axis=2, tiled=True)  102 us
    all_to_all x1, waiting for transfers between devices, body(): lax.all_to_all(updated, 'freq', split_axis=3, concat_axis=1, tiled=True)  88.4 us
    unnamed x35, local copies, waits for them, and re-layouts  39.8 us
    psum x1, waiting for transfers between devices, body(): model_re, model_im = lax.psum((model_re, model_im), 'rcv')  18 us
    another operation x1, local copies, waits for them, and re-layouts, body(): updated = jnp.stack([upd_re, upd_im], axis=0)  13.2 us
    dot_general x1, matrix products, body(): lax.dot_general(table, stacked, (((0,), (0,)), ((), ())), preferred_eleme...  12.1 us
    all_to_all x1, local copies, waits for them, and re-layouts, body(): lax.all_to_all(updated, 'freq', split_axis=3, concat_axis=1, tiled=True)  12 us
  transfers between devices with their start and end apart: 3, of which 3 were waited for; matrix products, arithmetic and copies ran while one was open for 1% of the time, Pallas kernels for 0%

commit v1 on v0

--- a/solution.py
+++ b/solution.py
@@ -53,7 +53,15 @@
     table = jnp.concatenate([jnp.cos(angle), -jnp.sin(angle)], axis=0).astype(jnp.bfloat16)
     level = threshold[0].astype(jnp.float32) / 64.0
     amplitude = math.sqrt(RCV / NF)
-    piece = lax.all_to_all(updated, "freq", split_axis=3, concat_axis=1, tiled=True)
+    ways, here = (lax.axis_size("freq"), lax.axis_index("freq"))
+    width_2 = updated.shape[3] // ways
+    turned = jnp.roll(updated, -here * width_2, axis=3)
+    got = [lax.slice_in_dim(turned, 0, width_2, axis=3)]
+    for far in range(1, ways):
+        sent = lax.slice_in_dim(turned, far * width_2, (far + 1) * width_2, axis=3)
+        got.append(lax.ppermute(sent, "freq", [(d, (d + far) % ways) for d in range(ways)]))
+    line = jnp.concatenate(got[::-1], axis=1)
+    piece = jnp.roll(line, (here + 1) * got[0].shape[1], axis=1)
     row_count = piece.shape[2]
     col_count = piece.shape[3]
     stacked = piece.reshape(2 * n_freq, row_count * col_count)

time: 537 us -> 490 us (0.912)
  local copies, waits for them, and re-layouts: 73.1 us -> 31.6 us
    all_to_all x1 -> x0, waiting for transfers between devices: 88.4 us -> none  [body(): lax.all_to_all(updated, 'freq', split_axis=3, concat_axis=1, tiled=True)]
    ppermute x0 -> x3, waiting for transfers between devices: none -> 83.9 us  [body(): lax.ppermute(sent, 'freq', [(d, (d + far) % ways) for d in range(ways)])]
    unnamed x35 -> x44, local copies, waits for them, and re-layouts: 39.8 us -> 21.3 us
    another operation x1 -> x0, local copies, waits for them, and re-layouts: 13.2 us -> none  [body(): updated = jnp.stack([upd_re, upd_im], axis=0)]
    all_to_all x1 -> x0, local copies, waits for them, and re-layouts: 12 us -> none  [body(): lax.all_to_all(updated, 'freq', split_axis=3, concat_axis=1, tiled=True)]
  transfers between devices with their start and end apart: 3 -> 5, of which waited for: 3 -> 4; matrix products, arithmetic and copies ran while one was open for 1% -> 1% of each run, Pallas kernels for 0% -> 0%
where the time goes in v1:
time: 490 us
  waiting for transfers between devices  204 us (42%)
  blocking collectives  196 us (40%)
  local copies, waits for them, and re-layouts  31.6 us (6%)
  matrix products  25.2 us (5%)
  between operations  15.7 us (3%)
  other arithmetic  12.6 us (3%)
    all_to_all x1, blocking collectives, body(): lax.all_to_all(sparse, 'freq', split_axis=0, concat_axis=2, tiled=True)  190 us
    all_gather x1, waiting for transfers between devices, body(): lax.all_gather(data, 'shot', axis=2, tiled=True)  102 us
    ppermute x3, waiting for transfers between devices, body(): lax.ppermute(sent, 'freq', [(d, (d + far) % ways) for d in range(ways)])  83.9 us
    unnamed x44, local copies, waits for them, and re-layouts  21.3 us
    psum x1, waiting for transfers between devices, body(): model_re, model_im = lax.psum((model_re, model_im), 'rcv')  18 us
    dot_general x1, matrix products, body(): lax.dot_general(table, stacked, (((0,), (0,)), ((), ())), preferred_eleme...  12.1 us
  transfers between devices with their start and end apart: 5, of which 4 were waited for; matrix products, arithmetic and copies ran while one was open for 1% of the time, Pallas kernels for 0%

profile of v1, /device:TPU:0, one launch (start us, length us, event | category | flops | bytes accessed | tf_op | source)
XLA Modules:
  0.0 489.5 jit_solution(1135150081969682364)
XLA Ops:
  6.5 0.0 copy-start.14
  6.5 0.0 all-gather.2.cloned.1.call-start
  6.5 0.7 all-gather.2.cloned.1.call-update
  7.3 0.0 all-reduce.4.cloned.1.call-start
  7.3 0.0 copy-done.14
  7.3 0.6 dynamic-slice
  8.6 0.0 copy-done.13
  8.6 0.2 dynamic-update-slice
  8.8 5.2 %all-reduce = s32[16]{0:T(128)S(1)} all-reduce(s32[16]{0:T(128)S(1)} %dynamic-update-slice), channel_id=1, replica_groups=mesh['grp'=2,'freq'=4,'shot'=2,'rcv'=2] {'shot'}, use_global_device_ids=true, to_apply=%add | all-reduce | flops 16 | bytes 128
  14.0 0.0 copy-done.12
  14.0 0.1 compare_convert_fusion
  14.1 101.5 %all-gather.2.cloned.1.call-done = bf16[2,64,16,2048]{3,2,1,0:T(8,128)(2,1)} async-done(((bf16[2,64,8,2048]{3,2,1,0:T(8,128)(2,1)}), bf16[2,64,16,2048]{3,2,1,0:T(8,128)(2,1)}) %all-gather.2.cloned.1.call-update) | async-done | bytes 8388624 | tf_op jit(solution)/shard_map/all_gather | solution.py:32
  115.6 5.3 %fusion = (bf16[64,16,2048]{2,1,0:T(8,128)(2,1)S(1)}, bf16[64,16,2048]{2,1,0:T(8,128)(2,1)S(1)}) fusion(bf16[2,64,16,2048]{3,2,1,0:T(8,128)(2,1)} %all-gather.2.cloned.1.call-done, f32[64]{0:T(128)S(1)} %get-tuple-element.16, f32[16,2048]{1,0:T(8,128)S(1)} %compare_convert_fusion, f32[64]{0:T(128)S(1)} %get-tuple-element.17), kind=kLoop, calls=%fused_computation.6 | loop fusion | flops 16777216 | bytes 16908800 | tf_op jit(solution)/shard_map/convert_element_type | solution.py:20
  121.0 0.0 copy-start
  121.0 0.0 copy-start.2
  121.0 0.0 copy-done.6
  121.0 1.6 fusion.7
  122.6 1.6 fusion.9
  124.1 0.0 copy-done
  124.1 1.9 fusion.28
  126.1 0.0 copy-done.2
  126.1 2.3 fusion.22
  128.4 0.0 all-reduce.4.cloned.1.call-update
  128.4 0.0 copy-done.10
  128.4 0.1 copy.13
  128.6 0.1 copy.12
  129.4 18.0 %all-reduce.4.cloned.1.call-done = (f32[64,8,16]{2,1,0:T(8,128)}, f32[64,8,16]{2,1,0:T(8,128)}) async-done(((f32[64,8,16]{2,1,0:T(8,128)}, f32[64,8,16]{2,1,0:T(8,128)}), (f32[64,8,16]{2,1,0:T(8,128)}, f32[64,8,16]{2,1,0:T(8,128)})) %all-reduce.4.cloned.1.call-update) | async-done | bytes 65552 | tf_op jit(solution)/shard_map/psum | solution.py:40
  147.3 3.1 fusion.46
  150.4 0.4 copy-done.3
  150.9 0.0 copy-done.9
  150.9 0.7 fusion.44
  151.6 1.5 copy-done.1
  153.1 1.3 copy-done.7
  154.3 1.0 fusion.6
  155.3 0.0 copy-done.8
  155.3 1.0 fusion.5
  156.3 2.4 fusion.3
  158.7 0.0 copy-start.4
  158.7 2.0 copy-done.4
  160.7 1.8 fusion.49
  162.5 3.7 collective-permute-start
  166.1 0.0 collective-permute-start.1
  166.1 1.0 collective-permute-start.2
  167.8 0.0 copy-start.5
  167.8 0.0 copy-done.11
  167.8 4.9 cosine_convert_fusion
  172.7 17.3 %collective-permute-done = bf16[2,64,8,512]{3,2,1,0:T(8,128)(2,1)S(1)} collective-permute-done((bf16[2,64,8,512]{3,2,1,0:T(8,128)(2,1)}, bf16[2,64,8,512]{3,2,1,0:T(8,128)(2,1)S(1)}, u32[]{:S(2)}, u32[]{:S(2)}) %collective-permute-start) | collective-permute-done | bytes 1048608 | tf_op jit(solution)/shard_map/ppermute | solution.py:62
  190.0 0.1 constant_dynamic-update-slice_fusion.5
  190.1 66.6 %collective-permute-done.1 = bf16[2,64,8,512]{3,2,1,0:T(8,128)(2,1)S(1)} collective-permute-done((bf16[2,64,8,512]{3,2,1,0:T(8,128)(2,1)}, bf16[2,64,8,512]{3,2,1,0:T(8,128)(2,1)S(1)}, u32[]{:S(2)}, u32[]{:S(2)}) %collective-permute-start.1) | collective-permute-done | bytes 1048608 | tf_op jit(solution)/shard_map/ppermute | solution.py:62
  256.7 0.1 constant_dynamic-update-slice_fusion.4
  256.8 0.0 collective-permute-done.2
  256.8 0.1 constant_dynamic-update-slice_fusion.3
  256.9 0.0 copy-done.5
  256.9 0.1 slice_dynamic-update-slice_fusion
  257.0 0.1 constant_dynamic-update-slice_fusion.2
  257.1 0.1 constant_dynamic-update-slice_fusion.1
  257.2 0.1 constant_dynamic-update-slice_fusion
  257.2 0.1 slice_dynamic-update-slice_fusion.1
  257.4 0.3 constant_dynamic-slice_fusion
  257.7 2.2 copy.14
  259.9 12.1 %multiply_convert_fusion = bf16[1024,4096]{1,0:T(8,128)(2,1)} fusion(bf16[512,4096]{1,0:T(8,128)(2,1)S(1)} %bitcast.77, f32[]{:T(128)} %bitcast.14, bf16[256,1024]{1,0:T(8,128)(2,1)S(1)} %get-tuple-element.15, bf16[256,1024]{1,0:T(8,128)(2,1)S(1)} %get-tuple-element.14), kind=kOutput, calls=%fused_computation | convolution fusion | flops 4326424576 | bytes 13631492 | tf_op jit(solution)/shard_map/dot_general | solution.py:69
  272.0 12.2 %copy.15 = bf16[128,8,8,512]{3,2,1,0:T(8,128)(2,1)} copy(bf16[128,8,8,512]{3,1,2,0:T(8,128)(2,1)} %bitcast.76) | data formatting | bytes 16777216
  284.2 190.4 %all_to_all.18 = bf16[1024,8,512]{2,1,0:T(8,128)(2,1)} all-to-all(bf16[1024,8,512]{2,1,0:T(8,128)(2,1)} %bitcast.73), channel_id=1, replica_groups=mesh['grp'=2,'freq'=4,'shot'=2,'rcv'=2] {'freq'}, dimensions={0} | all-to-all | bytes 16777216 | tf_op jit(solution)/shard_map/all_to_all | solution.py:76
  474.6 8.1 %copy.11 = bf16[4,256,8,512]{3,2,0,1:T(8,128)(2,1)} copy(bf16[4,256,8,512]{3,2,1,0:T(8,128)(2,1)} %bitcast.74) | data formatting | bytes 16777216 | tf_op jit(solution)/shard_map/all_to_all | solution.py:76
  (14 shorter events, 0.0 us)
Async XLA Ops:
  6.5 0.8 copy-start.14
  6.5 2.0 copy-start.13
  6.5 7.5 %copy-start.12 = (f32[2,64]{1,0:T(2,128)S(1)}, f32[2,64]{1,0:T(2,128)}, u32[]{:S(2)}) copy-start(f32[2,64]{1,0:T(2,128)} %param.11) | copy-start | bytes 1540
  6.5 109.1 %all-gather.2.cloned.1.call-start = ((), (), s32[]{:S(2)}) async-start(), calls=%async_computation.1 | async-start | bytes 12582912 | tf_op jit(solution)/shard_map/all_gather | solution.py:32
  7.3 140.1 %all-reduce.4.cloned.1.call-start = ((), (), s32[]{:S(2)}) async-start(), calls=%async_computation.2 | async-start | bytes 1048576 | tf_op jit(solution)/shard_map/psum | solution.py:40
  115.6 5.3 %copy-start.6 = (bf16[2,64,8,2048]{3,2,1,0:T(8,128)(2,1)S(1)}, bf16[2,64,8,2048]{3,2,1,0:T(8,128)(2,1)}, u32[]{:S(2)}) copy-start(bf16[2,64,8,2048]{3,2,1,0:T(8,128)(2,1)} %param.9) | copy-start | bytes 12582916
  121.0 3.2 copy-start
  121.0 5.1 %copy-start.2 = (bf16[64,16,2048]{2,1,0:T(8,128)(2,1)}, bf16[64,16,2048]{2,1,0:T(8,128)(2,1)S(1)}, u32[]{:S(2)}) copy-start(bf16[64,16,2048]{2,1,0:T(8,128)(2,1)S(1)} %get-tuple-element.8) | copy-start | bytes 12582916
  126.1 2.3 copy-start.10
  147.3 3.5 copy-start.3
  147.3 3.5 copy-start.9
  150.9 2.2 copy-start.1
  150.9 3.5 copy-start.7
  154.3 1.0 copy-start.8
  158.7 2.0 copy-start.4
  160.7 7.1 %copy-start.11 = (s32[256]{0:T(256)S(1)}, s32[256]{0:T(256)}, u32[]{:S(2)}) copy-start(s32[256]{0:T(256)} %param.13) | copy-start | bytes 3076
  162.5 27.6 %collective-permute-start = (bf16[2,64,8,512]{3,2,1,0:T(8,128)(2,1)}, bf16[2,64,8,512]{3,2,1,0:T(8,128)(2,1)S(1)}, u32[]{:S(2)}, u32[]{:S(2)}) collective-permute-start(bf16[2,64,8,512]{3,2,1,0:T(8,128)(2,1)} %get-tuple-element.11), channel_id=1, source_target_pairs={{0,12},{4,0},{8,4},{12,8},{1,13},{5,1},{9,5},{13,9},{2,14},{6,2},{... | collective-permute-start | bytes 3145736 | tf_op jit(solution)/shard_map/ppermute | solution.py:62
  166.1 90.6 %collective-permute-start.1 = (bf16[2,64,8,512]{3,2,1,0:T(8,128)(2,1)}, bf16[2,64,8,512]{3,2,1,0:T(8,128)(2,1)S(1)}, u32[]{:S(2)}, u32[]{:S(2)}) collective-permute-start(bf16[2,64,8,512]{3,2,1,0:T(8,128)(2,1)} %get-tuple-element.10), channel_id=1, source_target_pairs={{0,8},{4,12},{8,0},{12,4},{1,9},{5,13},{9,1},{13,5},{2,10},{6,14},... | collective-permute-start | bytes 3145736 | tf_op jit(solution)/shard_map/ppermute | solution.py:62
  166.1 90.7 %collective-permute-start.2 = (bf16[2,64,8,512]{3,2,1,0:T(8,128)(2,1)}, bf16[2,64,8,512]{3,2,1,0:T(8,128)(2,1)S(1)}, u32[]{:S(2)}, u32[]{:S(2)}) collective-permute-start(bf16[2,64,8,512]{3,2,1,0:T(8,128)(2,1)} %get-tuple-element.9), channel_id=1, source_target_pairs={{0,4},{4,8},{8,12},{12,0},{1,5},{5,9},{9,13},{13,1},{2,6},{6,10},{... | collective-permute-start | bytes 3145736 | tf_op jit(solution)/shard_map/ppermute | solution.py:62
  167.8 89.1 %copy-start.5 = (bf16[2,64,8,2048]{3,2,1,0:T(8,128)(2,1)S(1)}, bf16[2,64,8,2048]{3,2,1,0:T(8,128)(2,1)}, u32[]{:S(2)}) copy-start(bf16[2,64,8,2048]{3,2,1,0:T(8,128)(2,1)} %copy-done.4) | copy-start | bytes 12582916
Sparse Core Ops, SparseCore 0:
  8.9 106.6 all-gather.1
  128.5 18.7 all-reduce.3
